TPU v7x, 32 devices: a whole 2x2x4 slice. The times are simulated.
32 devices in a mesh: grp: 2 (over core), dev: 16 (over z, y, x).
Axes of the slice: x: 2, y: 2, z: 4, core: 2. Of those that a mesh axis runs over, the one named last changes fastest.
Arguments:
- state: float32 [2, 24, 24, 4096], P(None, None, None, ('grp', 'dev')), may hold values from -6 to 6
- hamiltonian: float32 [24, 24], replicated, may hold values from -1.2 to 1.2
- mode_rates: float32 [96], replicated, may hold values from 0.05 to 2
- ado_modes: int32 [3, 4096], P(None, ('grp', 'dev')), may hold values from 0 to 96
- link_src: int32 [8, 4096], P(None, ('grp', 'dev')), may hold values from 0 to 191, as said below
- link_site: int32 [8, 4096], P(None, ('grp', 'dev')), may hold values from 0 to 23
- link_coef: float32 [4, 8, 4096], P(None, None, ('grp', 'dev')), may hold values from -2.4 to 2.4
- send_ids: int32 [32, 64], P(('grp', 'dev')), may hold values from 0 to 127
- step_units: int32 [], replicated, may hold values from 12 to 16
Outputs:
- new_state: float32 [2, 24, 24, 4096], P(None, None, None, ('grp', 'dev'))
- error_norm: float32 [], replicated
Inputs may be any that keep to these rules, and one draw needn't show every extreme that they name: `link_src`: on each device every received position 128 to 191 is named by 1 to 4 couplings of that device's matrices, and some position by exactly 4.
All inputs are finite; a program needn't handle non-finite values.
Results may differ from a plain program's by a relative error of at most 0.0003.
Values sent between devices are 32-bit elements; how exact they have to be, the bound alone decides.
A program may use at most 128 MiB of HBM per device.

v0:
```python
import jax
import jax.numpy as jnp
from jax import lax
from jax.sharding import PartitionSpec as P

TABLEAU = (
    (0.2,),
    (3.0 / 40, 9.0 / 40),
    (44.0 / 45, -56.0 / 15, 32.0 / 9),
    (19372.0 / 6561, -25360.0 / 2187, 64448.0 / 6561, -212.0 / 729),
    (9017.0 / 3168, -355.0 / 33, 46732.0 / 5247, 49.0 / 176, -5103.0 / 18656),
    (35.0 / 384, 0.0, 500.0 / 1113, 125.0 / 192, -2187.0 / 6784, 11.0 / 84),
)
ERRORS = (71.0 / 57600, 0.0, -71.0 / 16695, 71.0 / 1920, -17253.0 / 339200, 22.0 / 525, -1.0 / 40)
ABS_TOL = 0.001
REL_TOL = 0.01
UNIT_STEP = 1.0 / 64
HIGHEST = lax.Precision.HIGHEST


def commute(symmetric, current):
    left_prod = jnp.einsum("ab,sbcx->sacx", symmetric, current, precision=HIGHEST)
    right_prod = jnp.einsum("sabx,bc->sacx", current, symmetric, precision=HIGHEST)
    return left_prod - right_prod


def decay_rates(ado_modes, mode_rates):
    extended = jnp.concatenate([mode_rates, jnp.zeros((1,), mode_rates.dtype)])
    levels = jnp.arange(extended.shape[0], dtype=jnp.int32)
    hits = (ado_modes[:, None, :] == levels[None, :, None]).astype(mode_rates.dtype)
    return jnp.sum(hits * extended[None, :, None], axis=(0, 1))


def selector(indices, count, dtype):
    levels = jnp.arange(count, dtype=jnp.int32)
    return (levels[:, None] == indices.reshape(-1)[None, :]).astype(dtype)


def masked_term(source, sites, coef):
    levels = jnp.arange(source.shape[1], dtype=jnp.int32)
    indicator = (levels[:, None] == sites[None, :]).astype(source.dtype)
    row_mask = indicator[:, None, :]
    column_mask = indicator[None, :, :]
    weight_real = coef[0] * row_mask - coef[2] * column_mask
    weight_imag = coef[1] * row_mask - coef[3] * column_mask
    real_part = weight_real * source[0] - weight_imag * source[1]
    imag_part = weight_real * source[1] + weight_imag * source[0]
    return jnp.stack([imag_part, -real_part])


def shards(
    state, hamiltonian, mode_rates, ado_modes, link_src, link_site, link_coef, send_ids, step_units
):
    outgoing = send_ids[0]
    symmetric = 0.5 * (hamiltonian + hamiltonian.T)
    decay = decay_rates(ado_modes, mode_rates)
    step_size = step_units.astype(state.dtype) * UNIT_STEP
    groups = lax.axis_size("grp")
    members = lax.axis_size("dev")
    sites = state.shape[1]
    owned = state.shape[3]
    received = outgoing.shape[0]
    links = link_src.shape[0]
    flat_rows = 2 * sites * sites
    pack_table = selector(outgoing, owned, state.dtype)
    link_table = selector(link_src, owned + received, state.dtype)

    def evaluate(current):
        flat_current = current.reshape(flat_rows, owned)
        packed = jnp.dot(flat_current, pack_table, precision=HIGHEST).reshape(
            2, sites, sites, received
        )
        commutator = commute(symmetric, current)
        total = jnp.stack([commutator[1], -commutator[0]]) - decay[None, None, None, :] * current
        moved = lax.all_to_all(packed, ("grp", "dev"), split_axis=3, concat_axis=3, tiled=True)
        combined = jnp.concatenate([flat_current, moved.reshape(flat_rows, received)], axis=1)
        fetched = jnp.dot(combined, link_table, precision=HIGHEST)
        for link in range(links):
            start = link * owned
            source = fetched[:, start : start + owned].reshape(2, sites, sites, owned)
            total = total + masked_term(source, link_site[link], link_coef[:, link])
        return total

    sections = [evaluate(state)]
    inner = state
    for weights in TABLEAU:
        inner = state
        for weight, section in zip(weights, sections):
            if weight != 0.0:
                inner = inner + step_size * weight * section
        sections.append(evaluate(inner))
    error = jnp.zeros_like(state)
    for weight, section in zip(ERRORS, sections):
        if weight != 0.0:
            error = error + step_size * weight * section
    scale = ABS_TOL + REL_TOL * jnp.maximum(jnp.abs(state), jnp.abs(inner))
    partial_sum = jnp.sum(jnp.square(error / scale))
    total_sum = lax.psum(partial_sum, ("grp", "dev"))
    entries = 2 * sites * sites * owned * groups * members
    return (inner, jnp.sqrt(total_sum / entries))


def solution(mesh):
    return jax.shard_map(
        shards,
        mesh=mesh,
        in_specs=(
            P(None, None, None, ("grp", "dev")),
            P(),
            P(),
            P(None, ("grp", "dev")),
            P(None, ("grp", "dev")),
            P(None, ("grp", "dev")),
            P(None, None, ("grp", "dev")),
            P(("grp", "dev"), None),
            P(),
        ),
        out_specs=(P(None, None, None, ("grp", "dev")), P()),
        check_vma=False,
    )
```

profile of v0, /device:TPU:0, one launch (start us, length us, event | category | flops | bytes accessed | tf_op | source)
XLA Modules:
  0.0 288.2 jit_solution(6076001582429804445)
XLA Ops:
  3.2 1.9 reshape.4447
  5.1 7.8 %all-to-all-start = ((f32[32,1,2304]{2,1,0:T(1,128)}), f32[32,1,2304]{2,1,0:T(1,128)S(1)}, u32[]{:S(2)}, u32[]{:S(2)}) async-start(f32[32,1,2304]{2,1,0:T(1,128)} %reshape.4447), calls=%async_computation | async-start | bytes 589824 | tf_op jit(solution)/shard_map/all_to_all | solution.py:75
  19.4 5.5 %all-to-all-done = f32[32,1,2304]{2,1,0:T(1,128)S(1)} async-done(((f32[32,1,2304]{2,1,0:T(1,128)}), f32[32,1,2304]{2,1,0:T(1,128)S(1)}, u32[]{:S(2)}, u32[]{:S(2)}) %all-to-all-start) | async-done | bytes 294944 | tf_op jit(solution)/shard_map/all_to_all | solution.py:75
  28.5 2.0 fusion.7
  37.4 1.9 reshape.4449
  39.3 2.8 all-to-all-start.1
  45.3 8.7 %all-to-all-done.1 = f32[32,1,2304]{2,1,0:T(1,128)S(1)} async-done(((f32[32,1,2304]{2,1,0:T(1,128)}), f32[32,1,2304]{2,1,0:T(1,128)S(1)}, u32[]{:S(2)}, u32[]{:S(2)}) %all-to-all-start.1) | async-done | bytes 294944 | tf_op jit(solution)/shard_map/all_to_all | solution.py:75
  54.0 2.1 reduce.1
  56.1 2.1 reshape.4450
  59.6 3.3 %fusion.11 = f32[1152,1024]{1,0:T(8,128)S(1)} fusion(f32[1152,64]{1,0:T(8,128)} %bitcast.356, f32[1152,128]{1,0:T(8,128)} %bitcast.351, s32[1024]{0:T(1024)S(1)} %bitcast.477), kind=kOutput, calls=%fused_computation.243 | convolution fusion | flops 2718326784 | bytes 5607424 | tf_op jit(solution)/shard_map/dot_general | solution.py:77
  69.6 3.3 %reshape.4451 = f32[32,1,2304]{2,1,0:T(1,128)} reshape(f32[64,2,24,24]{3,2,1,0:T(8,128)} %bitcast.340) | data formatting | bytes 589824
  72.9 3.5 %all-to-all-start.2 = ((f32[32,1,2304]{2,1,0:T(1,128)}), f32[32,1,2304]{2,1,0:T(1,128)}, u32[]{:S(2)}, u32[]{:S(2)}) async-start(f32[32,1,2304]{2,1,0:T(1,128)} %reshape.4451), calls=%async_computation.2 | async-start | bytes 589824 | tf_op jit(solution)/shard_map/all_to_all | solution.py:75
  77.9 10.4 %all-to-all-done.2 = f32[32,1,2304]{2,1,0:T(1,128)} async-done(((f32[32,1,2304]{2,1,0:T(1,128)}), f32[32,1,2304]{2,1,0:T(1,128)}, u32[]{:S(2)}, u32[]{:S(2)}) %all-to-all-start.2) | async-done | bytes 294944 | tf_op jit(solution)/shard_map/all_to_all | solution.py:75
  88.3 2.3 reduce.2
  90.6 2.3 reshape.4452
  93.0 2.0 copy.687
  94.9 2.0 fusion.15
  101.3 1.8 copy.726
  103.1 3.3 %reshape.4453 = f32[32,1,2304]{2,1,0:T(1,128)} reshape(f32[64,2,24,24]{3,2,1,0:T(8,128)} %bitcast.342) | data formatting | bytes 589824
  106.4 3.7 %all-to-all-start.3 = ((f32[32,1,2304]{2,1,0:T(1,128)}), f32[32,1,2304]{2,1,0:T(1,128)}, u32[]{:S(2)}, u32[]{:S(2)}) async-start(f32[32,1,2304]{2,1,0:T(1,128)} %reshape.4453), calls=%async_computation.3 | async-start | bytes 589824 | tf_op jit(solution)/shard_map/all_to_all | solution.py:75
  112.5 9.6 %all-to-all-done.3 = f32[32,1,2304]{2,1,0:T(1,128)} async-done(((f32[32,1,2304]{2,1,0:T(1,128)}), f32[32,1,2304]{2,1,0:T(1,128)}, u32[]{:S(2)}, u32[]{:S(2)}) %all-to-all-start.3) | async-done | bytes 294944 | tf_op jit(solution)/shard_map/all_to_all | solution.py:75
  122.0 2.3 reduce.3
  124.3 2.3 reshape.4454
  126.7 2.0 copy.727
  128.7 2.0 fusion.19
  137.6 3.3 %reshape.4455 = f32[32,1,2304]{2,1,0:T(1,128)} reshape(f32[64,2,24,24]{3,2,1,0:T(8,128)} %bitcast.344) | data formatting | bytes 589824
  141.0 3.5 %all-to-all-start.4 = ((f32[32,1,2304]{2,1,0:T(1,128)}), f32[32,1,2304]{2,1,0:T(1,128)}, u32[]{:S(2)}, u32[]{:S(2)}) async-start(f32[32,1,2304]{2,1,0:T(1,128)} %reshape.4455), calls=%async_computation.4 | async-start | bytes 589824 | tf_op jit(solution)/shard_map/all_to_all | solution.py:75
  146.8 9.6 %all-to-all-done.4 = f32[32,1,2304]{2,1,0:T(1,128)} async-done(((f32[32,1,2304]{2,1,0:T(1,128)}), f32[32,1,2304]{2,1,0:T(1,128)}, u32[]{:S(2)}, u32[]{:S(2)}) %all-to-all-start.4) | async-done | bytes 294944 | tf_op jit(solution)/shard_map/all_to_all | solution.py:75
  156.3 2.3 reduce.4
  158.7 2.3 reshape.4456
  161.0 2.0 copy.767
  163.0 2.0 fusion.23
  172.2 3.3 %reshape.4457 = f32[32,1,2304]{2,1,0:T(1,128)} reshape(f32[64,2,24,24]{3,2,1,0:T(8,128)} %bitcast.346) | data formatting | bytes 589824
  175.5 3.5 %all-to-all-start.5 = ((f32[32,1,2304]{2,1,0:T(1,128)}), f32[32,1,2304]{2,1,0:T(1,128)}, u32[]{:S(2)}, u32[]{:S(2)}) async-start(f32[32,1,2304]{2,1,0:T(1,128)} %reshape.4457), calls=%async_computation.5 | async-start | bytes 589824 | tf_op jit(solution)/shard_map/all_to_all | solution.py:75
  181.4 9.5 %all-to-all-done.5 = f32[32,1,2304]{2,1,0:T(1,128)} async-done(((f32[32,1,2304]{2,1,0:T(1,128)}), f32[32,1,2304]{2,1,0:T(1,128)}, u32[]{:S(2)}, u32[]{:S(2)}) %all-to-all-start.5) | async-done | bytes 294944 | tf_op jit(solution)/shard_map/all_to_all | solution.py:75
  190.9 3.0 %reduce.5 = f32[32,2304]{1,0:T(8,128)} reduce(f32[32,1,2304]{2,1,0:T(1,128)} %all-to-all-done.5, f32[]{:T(128)} %broadcast.2747), dimensions={1}, to_apply=%all_to_all.26.reduce_sub_computation | reduce | bytes 589828 | tf_op jit(solution)/shard_map/all_to_all | solution.py:75
  194.0 3.3 %reshape.4458 = f32[64,2,24,24]{3,2,1,0:T(8,128)} reshape(f32[32,2304]{1,0:T(8,128)} %reduce.5) | data formatting | bytes 589824
  197.3 2.8 copy.807
  200.1 3.1 %fusion.27 = f32[1152,1024]{1,0:T(8,128)S(1)} fusion(f32[1152,64]{1,0:T(8,128)} %bitcast.360, f32[1152,128]{1,0:T(8,128)S(1)} %bitcast.355, s32[1024]{0:T(1024)S(1)} %bitcast.481), kind=kOutput, calls=%fused_computation.259 | convolution fusion | flops 2718326784 | bytes 5607424 | tf_op jit(solution)/shard_map/dot_general | solution.py:77
  209.4 2.9 copy.845
  212.3 3.3 %reshape.4459 = f32[32,1,2304]{2,1,0:T(1,128)} reshape(f32[64,2,24,24]{3,2,1,0:T(8,128)} %bitcast.348) | data formatting | bytes 589824
  215.6 3.5 %all-to-all-start.6 = ((f32[32,1,2304]{2,1,0:T(1,128)}), f32[32,1,2304]{2,1,0:T(1,128)}, u32[]{:S(2)}, u32[]{:S(2)}) async-start(f32[32,1,2304]{2,1,0:T(1,128)} %reshape.4459), calls=%async_computation.6 | async-start | bytes 589824 | tf_op jit(solution)/shard_map/all_to_all | solution.py:75
  221.5 9.6 %all-to-all-done.6 = f32[32,1,2304]{2,1,0:T(1,128)} async-done(((f32[32,1,2304]{2,1,0:T(1,128)}), f32[32,1,2304]{2,1,0:T(1,128)}, u32[]{:S(2)}, u32[]{:S(2)}) %all-to-all-start.6) | async-done | bytes 294944 | tf_op jit(solution)/shard_map/all_to_all | solution.py:75
  231.1 3.0 %reduce.6 = f32[32,2304]{1,0:T(8,128)} reduce(f32[32,1,2304]{2,1,0:T(1,128)} %all-to-all-done.6, f32[]{:T(128)} %broadcast.2747), dimensions={1}, to_apply=%all_to_all.27.reduce_sub_computation | reduce | bytes 589828 | tf_op jit(solution)/shard_map/all_to_all | solution.py:75
  234.1 3.3 %reshape.4460 = f32[64,2,24,24]{3,2,1,0:T(8,128)} reshape(f32[32,2304]{1,0:T(8,128)} %reduce.6) | data formatting | bytes 589824
  237.5 2.8 copy.846
  240.3 3.1 %fusion.31 = f32[1152,1024]{1,0:T(8,128)S(1)} fusion(f32[1152,64]{1,0:T(8,128)} %bitcast.362, f32[1152,128]{1,0:T(8,128)S(1)} %bitcast.350, s32[1024]{0:T(1024)S(1)} %bitcast.482), kind=kOutput, calls=%fused_computation.263 | convolution fusion | flops 2718326784 | bytes 5607424 | tf_op jit(solution)/shard_map/dot_general | solution.py:77
  248.4 37.7 %psum.7 = f32[]{:T(128)} all-reduce(f32[]{:T(128)} %fusion.95), channel_id=1, replica_groups=mesh['grp'=2,'dev'=16] {'grp','dev'}, use_global_device_ids=true, to_apply=%region_2.0 | all-reduce | flops 1 | bytes 8 | tf_op jit(solution)/shard_map/psum | solution.py:98
  (654 shorter events, 68.0 us)
Async XLA Ops:
  3.2 9.8 %copy-start.260 = (f32[4,8,128]{2,1,0:T(8,128)S(1)}, f32[4,8,128]{2,1,0:T(8,128)}, u32[]{:S(2)}) copy-start(f32[4,8,128]{2,1,0:T(8,128)} %param.15) | copy-start | bytes 49156
  3.2 9.8 %copy-start.261 = (s32[8,128]{1,0:T(8,128)S(1)}, s32[8,128]{1,0:T(8,128)}, u32[]{:S(2)}) copy-start(s32[8,128]{1,0:T(8,128)} %param.14) | copy-start | bytes 12292
  3.2 9.9 %copy-start.246 = (f32[24,24]{1,0:T(8,128)S(1)}, f32[24,24]{1,0:T(8,128)}, u32[]{:S(2)}) copy-start(f32[24,24]{1,0:T(8,128)} %param.10) | copy-start | bytes 6916
  3.2 9.9 %copy-start = (f32[2,24,24,128]{3,2,1,0:T(8,128)S(1)}, f32[2,24,24,128]{3,2,1,0:T(8,128)}, u32[]{:S(2)}) copy-start(f32[2,24,24,128]{3,2,1,0:T(8,128)} %param.9) | copy-start | bytes 1769476
  3.2 10.6 %copy-start.263 = (f32[96]{0:T(128)S(1)}, f32[96]{0:T(128)}, u32[]{:S(2)}) copy-start(f32[96]{0:T(128)} %param.11) | copy-start | bytes 1156
  5.1 11.4 %copy-start.262 = (s32[3,128]{1,0:T(4,128)S(1)}, s32[3,128]{1,0:T(4,128)}, u32[]{:S(2)}) copy-start(s32[3,128]{1,0:T(4,128)} %param.12) | copy-start | bytes 4612
  5.1 19.7 %all-to-all-start = ((f32[32,1,2304]{2,1,0:T(1,128)}), f32[32,1,2304]{2,1,0:T(1,128)S(1)}, u32[]{:S(2)}, u32[]{:S(2)}) async-start(f32[32,1,2304]{2,1,0:T(1,128)} %reshape.4447), calls=%async_computation | async-start | bytes 589824 | tf_op jit(solution)/shard_map/all_to_all | solution.py:75
  26.7 1.8 copy-start.245
  30.6 0.9 copy-start.49
  30.6 0.9 copy-start.56
  30.6 0.9 copy-start.63
  32.6 1.0 copy-start.17
  32.7 1.1 copy-start.18
  32.7 1.1 copy-start.247
  39.3 14.7 %all-to-all-start.1 = ((f32[32,1,2304]{2,1,0:T(1,128)}), f32[32,1,2304]{2,1,0:T(1,128)S(1)}, u32[]{:S(2)}, u32[]{:S(2)}) async-start(f32[32,1,2304]{2,1,0:T(1,128)} %reshape.4449), calls=%async_computation.1 | async-start | bytes 589824 | tf_op jit(solution)/shard_map/all_to_all | solution.py:75
  65.0 1.0 copy-start.15
  65.0 1.1 copy-start.16
  65.0 1.1 copy-start.248
  66.1 1.2 copy-start.255
  72.9 15.4 %all-to-all-start.2 = ((f32[32,1,2304]{2,1,0:T(1,128)}), f32[32,1,2304]{2,1,0:T(1,128)}, u32[]{:S(2)}, u32[]{:S(2)}) async-start(f32[32,1,2304]{2,1,0:T(1,128)} %reshape.4451), calls=%async_computation.2 | async-start | bytes 589824 | tf_op jit(solution)/shard_map/all_to_all | solution.py:75
  99.1 1.1 copy-start.2
  99.1 1.1 copy-start.249
  106.4 15.6 %all-to-all-start.3 = ((f32[32,1,2304]{2,1,0:T(1,128)}), f32[32,1,2304]{2,1,0:T(1,128)}, u32[]{:S(2)}, u32[]{:S(2)}) async-start(f32[32,1,2304]{2,1,0:T(1,128)} %reshape.4453), calls=%async_computation.3 | async-start | bytes 589824 | tf_op jit(solution)/shard_map/all_to_all | solution.py:75
  132.8 1.1 copy-start.3
  132.8 1.1 copy-start.19
  132.8 1.2 copy-start.20
  132.8 1.2 copy-start.250
  134.0 1.3 copy-start.257
  141.0 15.4 %all-to-all-start.4 = ((f32[32,1,2304]{2,1,0:T(1,128)}), f32[32,1,2304]{2,1,0:T(1,128)}, u32[]{:S(2)}, u32[]{:S(2)}) async-start(f32[32,1,2304]{2,1,0:T(1,128)} %reshape.4455), calls=%async_computation.4 | async-start | bytes 589824 | tf_op jit(solution)/shard_map/all_to_all | solution.py:75
  167.0 1.1 copy-start.1
  167.0 1.2 copy-start.4
  167.0 1.3 copy-start.11
  167.0 1.4 copy-start.12
  167.0 1.4 copy-start.251
  168.4 1.5 copy-start.258
  175.5 15.4 %all-to-all-start.5 = ((f32[32,1,2304]{2,1,0:T(1,128)}), f32[32,1,2304]{2,1,0:T(1,128)}, u32[]{:S(2)}, u32[]{:S(2)}) async-start(f32[32,1,2304]{2,1,0:T(1,128)} %reshape.4457), calls=%async_computation.5 | async-start | bytes 589824 | tf_op jit(solution)/shard_map/all_to_all | solution.py:75
  205.2 1.1 copy-start.5
  205.2 1.1 copy-start.13
  205.2 1.2 copy-start.14
  205.2 1.2 copy-start.252
  206.4 1.6 copy-start.259
  208.1 32.2 %copy-start.7 = (f32[2,24,24,128]{3,2,1,0:T(8,128)}, f32[2,24,24,128]{3,2,1,0:T(8,128)S(1)}, u32[]{:S(2)}) copy-start(f32[2,24,24,128]{3,2,1,0:T(8,128)S(1)} %copy.880) | copy-start | bytes 1769476
  215.6 15.5 %all-to-all-start.6 = ((f32[32,1,2304]{2,1,0:T(1,128)}), f32[32,1,2304]{2,1,0:T(1,128)}, u32[]{:S(2)}, u32[]{:S(2)}) async-start(f32[32,1,2304]{2,1,0:T(1,128)} %reshape.4459), calls=%async_computation.6 | async-start | bytes 589824 | tf_op jit(solution)/shard_map/all_to_all | solution.py:75
  245.5 1.1 copy-start.6
  245.5 1.2 copy-start.8
  245.5 1.3 copy-start.9
  245.5 1.4 copy-start.10
  245.5 1.4 copy-start.253
  (223 other events, 166.6 us)
where the time goes:
time: 293 us; the launch traced here: 288 us
  local copies, waits for them, and re-layouts  79.8 us (27%)
  waiting for transfers between devices  62.8 us (21%)
  other arithmetic  40.2 us (14%)
  blocking collectives  37.7 us (13%)
  matrix products  33.1 us (11%)
  starting transfers between devices  28.3 us (10%)
  between operations  6.23 us (2%)
    all_to_all x7, waiting for transfers between devices, evaluate(): lax.all_to_all(packed, ('grp', 'dev'), split_axis=3, concat_axis=3, tiled...  62.8 us
    unnamed x544, local copies, waits for them, and re-layouts  48.1 us
    psum x1, blocking collectives, shards(): total_sum = lax.psum(partial_sum, ('grp', 'dev'))  37.7 us
    all_to_all x7, starting transfers between devices, evaluate(): lax.all_to_all(packed, ('grp', 'dev'), split_axis=3, concat_axis=3, tiled...  28.3 us
    dot_general x7, matrix products, evaluate(): fetched = jnp.dot(combined, link_table, precision=HIGHEST)  17.6 us
    all_to_all x7, other arithmetic, evaluate(): lax.all_to_all(packed, ('grp', 'dev'), split_axis=3, concat_axis=3, tiled...  16.4 us
    all_to_all x8, local copies, waits for them, and re-layouts, evaluate(): lax.all_to_all(packed, ('grp', 'dev'), split_axis=3, concat_axis=3, tiled...  14.1 us
    dot_general x7, local copies, waits for them, and re-layouts, evaluate(): jnp.dot(flat_current, pack_table, precision=HIGHEST)  12.3 us
  transfers between devices with their start and end apart: 7, of which 7 were waited for; matrix products, arithmetic and copies ran while one was open for 7% of the time, Pallas kernels for 0%

commit v1 on v0

v1 whole, which is shorter than its diff:
```python
import functools
from fractions import Fraction as Q

import jax
import jax.numpy as jnp
from jax import lax
from jax.experimental import pallas as pl
from jax.experimental.pallas import tpu as pltpu
from jax.sharding import PartitionSpec as P

TABLEAU = (
    (Q(1, 5),),
    (Q(3, 40), Q(9, 40)),
    (Q(44, 45), Q(-56, 15), Q(32, 9)),
    (Q(19372, 6561), Q(-25360, 2187), Q(64448, 6561), Q(-212, 729)),
    (Q(9017, 3168), Q(-355, 33), Q(46732, 5247), Q(49, 176), Q(-5103, 18656)),
    (Q(35, 384), Q(0), Q(500, 1113), Q(125, 192), Q(-2187, 6784), Q(11, 84)),
)
ERRORS = (Q(71, 57600), Q(0), Q(-71, 16695), Q(71, 1920), Q(-17253, 339200), Q(22, 525), Q(-1, 40))
ABS_TOL = 0.001
REL_TOL = 0.01
UNIT_STEP = 1.0 / 64
USES = 4
HIGHEST = lax.Precision.HIGHEST
MESH = pl.DeviceIdType.MESH
F32 = jnp.float32
BF16 = jnp.bfloat16


def step_polynomials():
    degree = len(ERRORS) + 1

    def combine(weights, sections, constant):
        total = [Q(constant)] + [Q(0)] * (degree - 1)
        for weight, section in zip(weights, sections):
            total = [t + weight * s for t, s in zip(total, section)]
        return total

    def advance(poly):
        return [Q(0)] + poly[:-1]

    sections = [advance(combine((), (), 1))]
    inner = None
    for weights in TABLEAU:
        inner = combine(weights, sections, 1)
        sections.append(advance(inner))
    error = combine(ERRORS, sections, 0)
    return [float(c) for c in inner], [float(c) for c in error]


NEW_POLY, ERR_POLY = step_polynomials()


def one_hot(condition, dtype):
    return jnp.where(condition, 1.0, 0.0).astype(dtype)


def iota(shape, dim):
    return lax.broadcasted_iota(jnp.int32, shape, dim)


def split(values):
    high = values.astype(BF16)
    return high, (values - high.astype(F32)).astype(BF16)


def dot(lhs, rhs):
    return jnp.dot(lhs, rhs, preferred_element_type=F32)


def dot_nt(lhs, rhs, precision=None):
    return lax.dot_general(
        lhs, rhs, (((1,), (1,)), ((), ())), precision=precision, preferred_element_type=F32
    )


def pick_scalar(index, table):
    value = jnp.float32(0.0)
    for place, entry in enumerate(table):
        if entry != 0.0:
            value = jnp.where(index == place, jnp.float32(entry), value)
    return value


def kernel(
    groups,
    members,
    state_ref,
    ham_ref,
    rates_ref,
    modes_ref,
    src_ref,
    site_ref,
    coef_ref,
    ids_ref,
    units_ref,
    out_ref,
    norm_ref,
    w_ref,
    err_ref,
    part_ref,
    super_ref,
    pick_ref,
    select_ref,
    request_ref,
    left_ref,
    right_ref,
    row_ref,
    col_ref,
    asked_row_ref,
    asked_col_ref,
    chosen_ref,
    cols_ref,
    halves_ref,
    fetched_ref,
    tl_ref,
    tr_ref,
    send_ref,
    recv_ref,
    send_sem,
    recv_sem,
):
    peers = groups * members
    sites = state_ref.shape[1]
    owned = state_ref.shape[3]
    links = src_ref.shape[0]
    received = ids_ref.shape[1]
    wide = links * owned
    asks = received * USES
    rows = asks // peers
    pairs = sites * sites
    width = send_ref.shape[1]
    my_grp, my_dev = lax.axis_index("grp"), lax.axis_index("dev")
    me = my_grp * members + my_dev

    def peer_id(step):
        peer = lax.rem(me + step, peers)
        return peer, (peer // members, lax.rem(peer, members))

    barrier = pltpu.get_barrier_semaphore()

    def greet(step, carry):
        _, target = peer_id(step)
        pl.semaphore_signal(barrier, inc=1, device_id=target, device_id_type=MESH)
        return carry

    lax.fori_loop(1, peers, greet, 0)

    def send_all(turn):
        def send(step, carry):
            peer, target = peer_id(step)
            pltpu.make_async_remote_copy(
                src_ref=send_ref.at[pl.ds(pl.multiple_of(peer * rows, rows), rows)],
                dst_ref=recv_ref.at[turn, pl.ds(pl.multiple_of(me * rows, rows), rows)],
                send_sem=send_sem.at[turn],
                recv_sem=recv_sem.at[turn],
                device_id=target,
                device_id_type=MESH,
            ).start()
            return carry

        lax.fori_loop(1, peers, send, 0)
        mine = pl.ds(pl.multiple_of(me * rows, rows), rows)
        recv_ref[turn, mine] = send_ref[mine]

    def bulk(turn, sem):
        every = pl.ds(0, (peers - 1) * rows)
        return pltpu.make_async_copy(send_ref.at[every], recv_ref.at[turn, every], sem.at[turn])

    def wait_all(turn):
        bulk(turn, recv_sem).wait()
        bulk(turn, send_sem).wait()

    step_size = units_ref[0, 0].astype(F32) * UNIT_STEP
    earlier = one_hot(iota((owned, owned), 0) < iota((owned, owned), 1), BF16)
    base = jnp.zeros((received, 1), F32)
    wanted = jnp.zeros((asks, owned), F32)
    for link in range(links):
        lanes = slice(link * owned, (link + 1) * owned)
        source = src_ref[link : link + 1, :]
        site = site_ref[link : link + 1, :]
        hit = iota((received, owned), 0) == source - owned
        hits = one_hot(hit, F32)
        before = dot(one_hot(hit, BF16), earlier) + base
        rank = jnp.sum(hits * before, axis=0, keepdims=True).astype(jnp.int32)
        base = base + jnp.sum(hits, axis=1, keepdims=True)
        ask = jnp.where(source >= owned, (source - owned) * USES + rank, -1)
        asking = iota((asks, owned), 0) == ask
        wanted = wanted + jnp.where(asking, site.astype(F32), 0.0)
        request_ref[:, lanes] = one_hot(asking, BF16)
        local = one_hot(iota((owned, owned), 0) == source, BF16)
        select_ref[:owned, lanes] = local
        select_ref[owned:, lanes] = local
    send_ref[...] = jnp.broadcast_to(jnp.sum(wanted, axis=1, keepdims=True), (asks, width))
    pl.semaphore_wait(barrier, peers - 1)
    send_all(0)

    for link in range(links):
        lanes = slice(link * owned, (link + 1) * owned)
        site = site_ref[link : link + 1, :]
        col_mask = one_hot(iota((sites, owned), 0) == site, F32)
        col_ref[:, lanes] = col_mask
        row_mask = one_hot(iota((sites, 1, owned), 0) == site[None], F32)
        row_ref[:, :, lanes] = row_mask
        for part in range(2):
            left = coef_ref[part, link : link + 1, :] * step_size
            right = coef_ref[part + 2, link : link + 1, :] * step_size
            left_ref[part, :, :, lanes] = row_mask * left[None]
            right_ref[part, :, lanes] = col_mask * right
    flat_coef = [
        jnp.concatenate([coef_ref[k, link : link + 1, :] for link in range(links)], axis=1)
        * step_size
        for k in range(4)
    ]
    first = one_hot(iota((sites, sites, sites), 0) == iota((sites, sites, sites), 2), F32)
    second = one_hot(iota((sites, sites, sites), 1) == iota((sites, sites, sites), 2), F32)
    first, second = first.reshape(pairs, sites), second.reshape(pairs, sites)
    ham = ham_ref[...] * (0.5 * step_size)

    def lifted(hot):
        half = jnp.dot(hot, ham, precision=HIGHEST, preferred_element_type=F32)
        half = half + dot_nt(hot, ham, HIGHEST)
        return dot_nt(half, hot, HIGHEST)

    same_first = dot_nt(first.astype(BF16), first.astype(BF16))
    same_second = dot_nt(second.astype(BF16), second.astype(BF16))
    operator = lifted(first) * same_second - lifted(second) * same_first
    high, low = split(operator)
    super_ref[:pairs] = high
    super_ref[pairs:] = low
    modes = rates_ref.shape[1]
    counts = jnp.zeros((modes, owned), F32)
    for depth in range(modes_ref.shape[0]):
        counts = counts + one_hot(iota((modes, owned), 0) == modes_ref[depth : depth + 1, :], F32)
    rates = jnp.broadcast_to(rates_ref[...], (8, modes))
    decay = jnp.dot(rates, counts, precision=HIGHEST, preferred_element_type=F32)[0:1] * step_size
    spread_low = iota((received, asks), 0) * USES
    spread_at = iota((received, asks), 1)
    spread = one_hot((spread_at >= spread_low) & (spread_at < spread_low + USES), BF16)
    ids = jnp.broadcast_to(ids_ref[...].astype(F32), (16, received)).astype(BF16)
    ids = dot(ids, spread)[0:1].astype(jnp.int32)
    picks = one_hot(iota((owned, asks), 0) == ids, BF16)
    pick_ref[:owned] = picks
    pick_ref[owned:] = picks
    w_ref[...] = state_ref[...]
    out_ref[...] = state_ref[...]
    err_ref[...] = jnp.zeros(err_ref.shape, F32)

    wait_all(0)
    asked = recv_ref[0].T[0:1].astype(jnp.int32)
    asked_col_ref[...] = one_hot(iota((sites, asks), 0) == asked, F32)
    asked_row_ref[...] = one_hot(iota((sites, 1, asks), 0) == asked[None], F32)

    def advance(turn, carry):
        high, low = split(w_ref[...].reshape(2 * pairs, owned))
        halves_ref[...] = jnp.concatenate([high, low], axis=1)
        chosen_ref[...] = dot(halves_ref[...], pick_ref[...]).reshape(2, sites, sites, asks)

        def extract(row, total):
            block = chosen_ref[:, row]
            cols_ref[:, pl.ds(row, 1), :] = jnp.sum(
                block * asked_col_ref[...][None], axis=1, keepdims=True
            )
            return total + block * asked_row_ref[row][None]

        picked = lax.fori_loop(0, sites, extract, jnp.zeros((2, sites, asks), F32))
        outgoing = jnp.concatenate(
            [
                picked.reshape(2 * sites, asks),
                cols_ref[...].reshape(2 * sites, asks),
                jnp.zeros((width - 4 * sites, asks), F32),
            ],
            axis=0,
        )
        send_ref[...] = outgoing.T
        send_all(turn)

        fetched_ref[...] = dot(halves_ref[...], select_ref[...]).reshape(2, sites, sites, wide)
        high = jnp.concatenate([halves_ref[:pairs, :owned], halves_ref[pairs:, :owned]], axis=1)
        low = jnp.concatenate([halves_ref[:pairs, owned:], halves_ref[pairs:, owned:]], axis=1)
        both = dot(super_ref[...], high)
        bracket = both[:pairs] + both[pairs:] + dot(super_ref[:pairs], low)
        part_ref[0] = bracket[:, owned:].reshape(sites, sites, owned) - decay * w_ref[0]
        part_ref[1] = -bracket[:, :owned].reshape(sites, sites, owned) - decay * w_ref[1]

        def near(row, carry):
            real, imag = part_ref[0, row], part_ref[1, row]
            for link in range(links):
                lanes = slice(link * owned, (link + 1) * owned)
                weight_real = left_ref[0, row, :, lanes] - right_ref[0, :, lanes]
                weight_imag = left_ref[1, row, :, lanes] - right_ref[1, :, lanes]
                source_real = fetched_ref[0, row, :, lanes]
                source_imag = fetched_ref[1, row, :, lanes]
                real = real + weight_real * source_imag + weight_imag * source_real
                imag = imag + weight_imag * source_imag - weight_real * source_real
            part_ref[0, row] = real
            part_ref[1, row] = imag
            return carry

        lax.fori_loop(0, sites, near, 0)

        wait_all(turn)
        high, low = split(recv_ref[turn].T)
        found = dot(jnp.concatenate([high, low], axis=0), request_ref[...])
        found = found[:width] + found[width:]
        row_real, row_imag = found[:sites], found[sites : 2 * sites]
        col_real, col_imag = found[2 * sites : 3 * sites], found[3 * sites : 4 * sites]
        left_real, left_imag, right_real, right_imag = flat_coef
        tl_ref[0] = left_real * row_imag + left_imag * row_real
        tl_ref[1] = left_imag * row_imag - left_real * row_real
        tr_ref[0] = -(right_real * col_imag + right_imag * col_real)[:, None, :]
        tr_ref[1] = (right_real * col_real - right_imag * col_imag)[:, None, :]
        new_weight = pick_scalar(turn, NEW_POLY)
        err_weight = pick_scalar(turn, ERR_POLY)

        def far(row, carry):
            for part in range(2):
                value = part_ref[part, row]
                for link in range(links):
                    lanes = slice(link * owned, (link + 1) * owned)
                    value = value + row_ref[row, :, lanes] * tl_ref[part, :, lanes]
                    value = value + col_ref[:, lanes] * tr_ref[part, row, :, lanes]
                w_ref[part, row] = value
                out_ref[part, row] = out_ref[part, row] + new_weight * value
                err_ref[part, row] = err_ref[part, row] + err_weight * value
            return carry

        lax.fori_loop(0, sites, far, 0)
        return carry

    turns = len(ERRORS)
    lax.fori_loop(1, turns + 1, advance, 0)

    scale = ABS_TOL + REL_TOL * jnp.maximum(jnp.abs(state_ref[...]), jnp.abs(out_ref[...]))
    ratio = err_ref[...] / scale
    tile = jnp.sum((ratio * ratio).reshape(2 * pairs // 8, 8, owned), axis=0)
    tile = jnp.sum(tile, axis=0, keepdims=True)
    tile = jnp.sum(tile, axis=1, keepdims=True)
    send_ref[...] = jnp.broadcast_to(tile, (asks, width))
    last = turns + 1
    send_all(last)
    wait_all(last)
    total = jnp.sum(recv_ref[last], axis=0, keepdims=True) * (1.0 / rows)
    entries = 2 * pairs * owned * peers
    norm_ref[...] = jnp.broadcast_to(jnp.sqrt(total[:, :128] / entries), norm_ref.shape)


def shards(
    state, hamiltonian, mode_rates, ado_modes, link_src, link_site, link_coef, send_ids, step_units
):
    groups = lax.axis_size("grp")
    members = lax.axis_size("dev")
    sites, owned = state.shape[1], state.shape[3]
    links = link_src.shape[0]
    received = send_ids.shape[1]
    asks = received * USES
    wide = links * owned
    pairs = sites * sites
    width = -(-4 * sites // 128) * 128
    turns = len(ERRORS) + 2
    vmem = pl.BlockSpec(memory_space=pltpu.VMEM)
    new_state, norm = pl.pallas_call(
        functools.partial(kernel, groups, members),
        out_shape=(
            jax.ShapeDtypeStruct(state.shape, F32),
            jax.ShapeDtypeStruct((8, 128), F32),
        ),
        in_specs=[vmem] * 8 + [pl.BlockSpec(memory_space=pltpu.SMEM)],
        out_specs=(vmem, vmem),
        scratch_shapes=[
            pltpu.VMEM(state.shape, F32),
            pltpu.VMEM(state.shape, F32),
            pltpu.VMEM(state.shape, F32),
            pltpu.VMEM((2 * pairs, pairs), BF16),
            pltpu.VMEM((2 * owned, asks), BF16),
            pltpu.VMEM((2 * owned, wide), BF16),
            pltpu.VMEM((asks, wide), BF16),
            pltpu.VMEM((2, sites, 1, wide), F32),
            pltpu.VMEM((2, sites, wide), F32),
            pltpu.VMEM((sites, 1, wide), F32),
            pltpu.VMEM((sites, wide), F32),
            pltpu.VMEM((sites, 1, asks), F32),
            pltpu.VMEM((sites, asks), F32),
            pltpu.VMEM((2, sites, sites, asks), F32),
            pltpu.VMEM((2, sites, asks), F32),
            pltpu.VMEM((2 * pairs, 2 * owned), BF16),
            pltpu.VMEM((2, sites, sites, wide), F32),
            pltpu.VMEM((2, sites, wide), F32),
            pltpu.VMEM((2, sites, 1, wide), F32),
            pltpu.VMEM((asks, width), F32),
            pltpu.VMEM((turns, asks, width), F32),
            pltpu.SemaphoreType.DMA((turns,)),
            pltpu.SemaphoreType.DMA((turns,)),
        ],
        compiler_params=pltpu.CompilerParams(
            collective_id=0, has_side_effects=True, vmem_limit_bytes=48 * 1024 * 1024
        ),
    )(
        state,
        hamiltonian,
        mode_rates.reshape(1, -1),
        ado_modes,
        link_src,
        link_site,
        link_coef,
        send_ids,
        step_units.reshape(1, 1),
    )
    return new_state, norm[0, 0]


def solution(mesh):
    return jax.shard_map(
        shards,
        mesh=mesh,
        in_specs=(
            P(None, None, None, ("grp", "dev")),
            P(),
            P(),
            P(None, ("grp", "dev")),
            P(None, ("grp", "dev")),
            P(None, ("grp", "dev")),
            P(None, None, ("grp", "dev")),
            P(("grp", "dev"), None),
            P(),
        ),
        out_specs=(P(None, None, None, ("grp", "dev")), P()),
        check_vma=False,
    )
```

time: 293 us -> 81.9 us (0.28); the launches traced: 288 us -> 81.4 us
  Pallas kernels: 0 us -> 74.3 us
  local copies, waits for them, and re-layouts: 79.8 us -> 5.83 us
  waiting for transfers between devices: 62.8 us -> 0 us
  other arithmetic: 40.2 us -> 0 us
  blocking collectives: 37.7 us -> 0 us
  matrix products: 33.1 us -> 0 us
  starting transfers between devices: 28.3 us -> 0 us
  between operations: 6.23 us -> 1.34 us
    pallas_call x0 -> x1, Pallas kernels: none -> 74.3 us  [shards(): pl.pallas_call(functools.partial(kernel, groups, members), out_shape=(jax...]
    all_to_all x7 -> x0, waiting for transfers between devices: 62.8 us -> none  [evaluate(): lax.all_to_all(packed, ('grp', 'dev'), split_axis=3, concat_axis=3, tiled...]
    unnamed x544 -> x17, local copies, waits for them, and re-layouts: 48.1 us -> 5.32 us
    psum x1 -> x0, blocking collectives: 37.7 us -> none  [shards(): total_sum = lax.psum(partial_sum, ('grp', 'dev'))]
    dot_general x28 -> x0, matrix products: 33.1 us -> none  [the longest x7 17.6 us: evaluate(): fetched = jnp.dot(combined, link_table, precision=HIGHEST)]
    all_to_all x7 -> x0, starting transfers between devices: 28.3 us -> none  [evaluate(): lax.all_to_all(packed, ('grp', 'dev'), split_axis=3, concat_axis=3, tiled...]
    all_to_all x7 -> x0, other arithmetic: 16.4 us -> none  [evaluate(): lax.all_to_all(packed, ('grp', 'dev'), split_axis=3, concat_axis=3, tiled...]
    all_to_all x8 -> x0, local copies, waits for them, and re-layouts: 14.1 us -> none  [evaluate(): lax.all_to_all(packed, ('grp', 'dev'), split_axis=3, concat_axis=3, tiled...]
  transfers between devices with their start and end apart: 7 -> 0, of which waited for: 7 -> 0; matrix products, arithmetic and copies ran while one was open for 7% -> 0% of each run, Pallas kernels for 0% -> 0%
where the time goes in v1:
time: 81.9 us; the launch traced here: 81.4 us
  Pallas kernels  74.3 us (91%)
  local copies, waits for them, and re-layouts  5.83 us (7%)
  between operations  1.34 us (2%)
    pallas_call x1, Pallas kernels, shards(): pl.pallas_call(functools.partial(kernel, groups, members), out_shape=(jax...  74.3 us
    unnamed x17, local copies, waits for them, and re-layouts  5.32 us

profile of v1, /device:TPU:0, one launch (start us, length us, event | category | flops | bytes accessed | tf_op | source)
XLA Modules:
  0.0 81.4 jit_solution(17605023191791450116)
XLA Ops:
  0.6 0.0 copy-start.3
  1.3 0.0 copy-start.6
  1.3 0.0 copy-start.7
  1.3 0.0 copy-done.3
  1.3 0.6 copy-done.6
  2.0 0.0 copy-done.7
  2.0 0.0 copy-start
  2.0 1.1 %copy-done = f32[2,24,24,128]{3,2,1,0:T(8,128)S(1)} copy-done((f32[2,24,24,128]{3,2,1,0:T(8,128)S(1)}, f32[2,24,24,128]{3,2,1,0:T(8,128)}, u32[]{:S(2)}) %copy-start) | copy-done | bytes 589848
  3.0 0.0 copy-start.1
  3.0 0.7 copy-done.1
  3.8 0.0 copy-start.2
  3.8 0.7 copy-done.2
  4.5 0.0 copy-start.4
  4.5 0.7 copy-done.4
  5.2 0.0 copy-start.5
  5.2 0.7 copy-done.5
  5.8 74.3 %shard_map.104 = (f32[2,24,24,128]{3,2,1,0:T(8,128)S(1)}, f32[8,128]{1,0:T(8,128)S(1)}) custom-call(f32[2,24,24,128]{3,2,1,0:T(8,128)S(1)} %copy-done, f32[24,24]{1,0:T(8,128)S(1)} %copy-done.2, f32[1,96]{1,0:T(1,128)S(1)} %bitcast.4, s32[3,128]{1,0:T(4,128)S(1)} %copy-done.5, s32[8,128]{1,0:T(8,128)S(1)} %copy-done.3, s32[8,128]{1,0:T(8,128)S(1)} %copy-done.4, ...), custom_call_target="tpu_custom_call" | custom-call | tf_op jit(solution)/shard_map/pallas_call | solution.py:362
  80.1 0.5 slice.3
  80.6 0.8 %copy.13 = f32[2,24,24,128]{3,2,1,0:T(8,128)} copy(f32[2,24,24,128]{3,2,1,0:T(8,128)S(1)} %get-tuple-element.8) | data formatting | bytes 1179648
Async XLA Ops:
  0.6 0.7 copy-start.3
  1.3 0.7 copy-start.6
  1.3 0.7 copy-start.7
  2.0 1.1 %copy-start = (f32[2,24,24,128]{3,2,1,0:T(8,128)S(1)}, f32[2,24,24,128]{3,2,1,0:T(8,128)}, u32[]{:S(2)}) copy-start(f32[2,24,24,128]{3,2,1,0:T(8,128)} %state_ref.1) | copy-start | bytes 1769476
  3.0 0.7 copy-start.1
  3.8 0.7 copy-start.2
  4.5 0.7 copy-start.4
  5.2 0.7 copy-start.5

commit v2 on v1

v2 whole, which is shorter than its diff:
```python
import functools
from fractions import Fraction as Q

import jax
import jax.numpy as jnp
from jax import lax
from jax.experimental import pallas as pl
from jax.experimental.pallas import tpu as pltpu
from jax.sharding import PartitionSpec as P

TABLEAU = (
    (Q(1, 5),),
    (Q(3, 40), Q(9, 40)),
    (Q(44, 45), Q(-56, 15), Q(32, 9)),
    (Q(19372, 6561), Q(-25360, 2187), Q(64448, 6561), Q(-212, 729)),
    (Q(9017, 3168), Q(-355, 33), Q(46732, 5247), Q(49, 176), Q(-5103, 18656)),
    (Q(35, 384), Q(0), Q(500, 1113), Q(125, 192), Q(-2187, 6784), Q(11, 84)),
)
ERRORS = (Q(71, 57600), Q(0), Q(-71, 16695), Q(71, 1920), Q(-17253, 339200), Q(22, 525), Q(-1, 40))
ABS_TOL = 0.001
REL_TOL = 0.01
UNIT_STEP = 1.0 / 64
USES = 4
HIGHEST = lax.Precision.HIGHEST
MESH = pl.DeviceIdType.MESH
F32 = jnp.float32
BF16 = jnp.bfloat16


def step_polynomials():
    degree = len(ERRORS) + 1

    def combine(weights, sections, constant):
        total = [Q(constant)] + [Q(0)] * (degree - 1)
        for weight, section in zip(weights, sections):
            total = [t + weight * s for t, s in zip(total, section)]
        return total

    def advance(poly):
        return [Q(0)] + poly[:-1]

    sections = [advance(combine((), (), 1))]
    inner = None
    for weights in TABLEAU:
        inner = combine(weights, sections, 1)
        sections.append(advance(inner))
    error = combine(ERRORS, sections, 0)
    return [float(c) for c in inner], [float(c) for c in error]


NEW_POLY, ERR_POLY = step_polynomials()


def one_hot(condition, dtype):
    return jnp.where(condition, 1.0, 0.0).astype(dtype)


def iota(shape, dim):
    return lax.broadcasted_iota(jnp.int32, shape, dim)


def split(values):
    high = values.astype(BF16)
    return high, (values - high.astype(F32)).astype(BF16)


def dot(lhs, rhs):
    return jnp.dot(lhs, rhs, preferred_element_type=F32)


def dot_nt(lhs, rhs, precision=None):
    return lax.dot_general(
        lhs, rhs, (((1,), (1,)), ((), ())), precision=precision, preferred_element_type=F32
    )


def kernel(
    groups,
    members,
    state_hbm,
    ham_hbm,
    rates_hbm,
    modes_hbm,
    src_hbm,
    site_hbm,
    coef_hbm,
    ids_hbm,
    units_hbm,
    out_ref,
    norm_ref,
    ham_ref,
    rates_ref,
    modes_ref,
    src_ref,
    site_ref,
    coef_ref,
    ids_ref,
    units_ref,
    power_ref,
    part_ref,
    super_ref,
    pick_ref,
    select_ref,
    request_ref,
    place_ref,
    weight_ref,
    own_row_ref,
    own_col_ref,
    asked_row_ref,
    asked_col_ref,
    chosen_ref,
    cols_ref,
    halves_ref,
    fetched_ref,
    tr_ref,
    send_ref,
    recv_ref,
    load_sem,
    send_sem,
    recv_sem,
):
    peers = groups * members
    sites = state_hbm.shape[1]
    owned = state_hbm.shape[3]
    links = src_ref.shape[0]
    received = ids_ref.shape[1]
    wide = links * owned
    asks = received * USES
    rows = asks // peers
    pairs = sites * sites
    width = send_ref.shape[1]
    my_grp, my_dev = lax.axis_index("grp"), lax.axis_index("dev")
    me = my_grp * members + my_dev

    def wrap(value, size):
        return jnp.where(value >= size, value - size, value)

    def each_peer(visit):
        for jump in range(1, groups):
            visit(wrap(my_grp + jump, groups), my_dev)

        def ring(step, carry):
            dev = wrap(my_dev + step, members)
            for jump in range(groups):
                visit(wrap(my_grp + jump, groups), dev)
            return carry

        lax.fori_loop(1, members, ring, 0)

    barrier = pltpu.get_barrier_semaphore()

    def greet(grp, dev):
        pl.semaphore_signal(barrier, inc=1, device_id=(grp, dev), device_id_type=MESH)

    loads = [
        pltpu.make_async_copy(source, target, load_sem.at[place])
        for place, (source, target) in enumerate(
            (
                (src_hbm, src_ref),
                (site_hbm, site_ref),
                (coef_hbm, coef_ref),
                (units_hbm, units_ref),
                (ham_hbm, ham_ref),
                (rates_hbm, rates_ref),
                (modes_hbm, modes_ref),
                (ids_hbm, ids_ref),
                (state_hbm, power_ref.at[0]),
            )
        )
    ]
    for load in loads:
        load.start()
    each_peer(greet)

    def send_all(turn):
        mine = pl.ds(pl.multiple_of(me * rows, rows), rows)

        def send(grp, dev):
            peer = grp * members + dev
            pltpu.make_async_remote_copy(
                src_ref=send_ref.at[pl.ds(pl.multiple_of(peer * rows, rows), rows)],
                dst_ref=recv_ref.at[turn, mine],
                send_sem=send_sem.at[turn],
                recv_sem=recv_sem.at[turn],
                device_id=(grp, dev),
                device_id_type=MESH,
            ).start()

        each_peer(send)
        recv_ref[turn, mine] = send_ref[mine]

    def bulk(turn, sem):
        every = pl.ds(0, (peers - 1) * rows)
        return pltpu.make_async_copy(send_ref.at[every], recv_ref.at[turn, every], sem.at[turn])

    def wait_all(turn):
        bulk(turn, recv_sem).wait()
        bulk(turn, send_sem).wait()

    earlier = one_hot(iota((owned, owned), 0) < iota((owned, owned), 1), BF16)
    base = jnp.zeros((received, 1), F32)
    wanted = jnp.zeros((asks, owned), F32)
    place = jnp.zeros((asks, owned), F32)
    loads[0].wait()
    loads[1].wait()
    for link in range(links):
        lanes = slice(link * owned, (link + 1) * owned)
        source = src_ref[link : link + 1, :]
        site = site_ref[link : link + 1, :]
        hit = iota((received, owned), 0) == source - owned
        hits = one_hot(hit, F32)
        before = dot(one_hot(hit, BF16), earlier) + base
        rank = jnp.sum(hits * before, axis=0, keepdims=True).astype(jnp.int32)
        base = base + jnp.sum(hits, axis=1, keepdims=True)
        ask = jnp.where(source >= owned, (source - owned) * USES + rank, -1)
        asking = iota((asks, owned), 0) == ask
        wanted = wanted + jnp.where(asking, site.astype(F32), 0.0)
        request = one_hot(asking, F32)
        request_ref[:, lanes] = request
        place = place + request
        local = one_hot(iota((owned, owned), 0) == source, BF16)
        select_ref[:owned, lanes] = local
        select_ref[owned:, lanes] = local
    send_ref[...] = jnp.broadcast_to(jnp.sum(wanted, axis=1, keepdims=True), (asks, width))
    pl.semaphore_wait(barrier, peers - 1)
    send_all(0)

    place_ref[:asks] = place.astype(BF16)
    place_ref[asks:] = place.astype(BF16)
    for load in loads[2:]:
        load.wait()
    step_size = units_ref[0, 0].astype(F32) * UNIT_STEP

    def flat(ref):
        return jnp.concatenate([ref[link : link + 1, :] for link in range(links)], axis=1)

    table = [flat(coef_ref.at[k]) * step_size for k in range(4)]
    table = table + [flat(site_ref).astype(F32), jnp.zeros((3, wide), F32)]
    table = dot_nt(jnp.concatenate(table, axis=0), request_ref[...], HIGHEST)
    left_real, left_imag = table[0:1], table[1:2]
    right_real, right_imag = table[2:3], table[3:4]
    own_site = jnp.round(table[4:5]).astype(jnp.int32)
    own_col_ref[...] = one_hot(iota((sites, asks), 0) == own_site, F32)
    own_row_ref[...] = one_hot(iota((sites, 1, asks), 0) == own_site[None], F32)
    for link in range(links):
        lanes = slice(link * owned, (link + 1) * owned)
        site = site_ref[link : link + 1, :]
        for part in range(2):
            left = coef_ref[part, link : link + 1, :] * step_size
            right = coef_ref[part + 2, link : link + 1, :] * step_size
            right = jnp.where(iota((sites, owned), 0) == site, right, 0.0)
            for row in range(sites):
                weight_ref[part, row, :, lanes] = jnp.where(site == row, left, 0.0) - right
    first = one_hot(iota((sites, sites, sites), 0) == iota((sites, sites, sites), 2), F32)
    second = one_hot(iota((sites, sites, sites), 1) == iota((sites, sites, sites), 2), F32)
    first, second = first.reshape(pairs, sites), second.reshape(pairs, sites)
    ham = ham_ref[...] * (0.5 * step_size)

    def lifted(hot):
        half = jnp.dot(hot, ham, precision=HIGHEST, preferred_element_type=F32)
        half = half + dot_nt(hot, ham, HIGHEST)
        return dot_nt(half, hot, HIGHEST)

    same_first = dot_nt(first.astype(BF16), first.astype(BF16))
    same_second = dot_nt(second.astype(BF16), second.astype(BF16))
    operator = lifted(first) * same_second - lifted(second) * same_first
    high, low = split(operator)
    super_ref[:pairs] = high
    super_ref[pairs:] = low
    modes = rates_ref.shape[1]
    counts = jnp.zeros((modes, owned), F32)
    for depth in range(modes_ref.shape[0]):
        counts = counts + one_hot(iota((modes, owned), 0) == modes_ref[depth : depth + 1, :], F32)
    rates = jnp.broadcast_to(rates_ref[...], (8, modes))
    decay = jnp.dot(rates, counts, precision=HIGHEST, preferred_element_type=F32)[0:1] * step_size
    spread_low = iota((received, asks), 0) * USES
    spread_at = iota((received, asks), 1)
    spread = one_hot((spread_at >= spread_low) & (spread_at < spread_low + USES), BF16)
    ids = jnp.broadcast_to(ids_ref[...].astype(F32), (16, received)).astype(BF16)
    ids = dot(ids, spread)[0:1].astype(jnp.int32)
    picks = one_hot(iota((owned, asks), 0) == ids, BF16)
    pick_ref[:owned] = picks
    pick_ref[owned:] = picks

    wait_all(0)
    asked = recv_ref[0].T[0:1].astype(jnp.int32)
    asked_col_ref[...] = one_hot(iota((sites, asks), 0) == asked, F32)
    asked_row_ref[...] = one_hot(iota((sites, 1, asks), 0) == asked[None], F32)

    def advance(turn, carry):
        before = turn - 1
        high, low = split(power_ref[before].reshape(2 * pairs, owned))
        halves_ref[...] = jnp.concatenate([high, low], axis=1)
        chosen_ref[...] = dot(halves_ref[...], pick_ref[...]).reshape(2, sites, sites, asks)
        col_mask = asked_col_ref[...]
        picked = []
        for part in range(2):
            total = jnp.zeros((sites, asks), F32)
            for row in range(sites):
                block = chosen_ref[part, row]
                total = total + block * asked_row_ref[row]
                cols_ref[part, row : row + 1, :] = jnp.sum(block * col_mask, axis=0, keepdims=True)
            picked.append(total)
        outgoing = jnp.concatenate(
            picked
            + [cols_ref[...].reshape(2 * sites, asks), jnp.zeros((width - 4 * sites, asks), F32)],
            axis=0,
        )
        send_ref[...] = outgoing.T
        send_all(turn)

        fetched_ref[...] = dot(halves_ref[...], select_ref[...]).reshape(2, sites, sites, wide)
        high = jnp.concatenate([halves_ref[:pairs, :owned], halves_ref[pairs:, :owned]], axis=1)
        low = jnp.concatenate([halves_ref[:pairs, owned:], halves_ref[pairs:, owned:]], axis=1)
        both = dot(super_ref[...], high)
        bracket = both[:pairs] + both[pairs:] + dot(super_ref[:pairs], low)
        part_ref[0] = (
            bracket[:, owned:].reshape(sites, sites, owned) - decay * power_ref[before, 0]
        )
        part_ref[1] = (
            -bracket[:, :owned].reshape(sites, sites, owned) - decay * power_ref[before, 1]
        )

        def near(row, carry):
            real, imag = part_ref[0, row], part_ref[1, row]
            for link in range(links):
                lanes = slice(link * owned, (link + 1) * owned)
                weight_real, weight_imag = (weight_ref[k, row, :, lanes] for k in range(2))
                source_real, source_imag = (fetched_ref[k, row, :, lanes] for k in range(2))
                real = real + (weight_real * source_imag + weight_imag * source_real)
                imag = imag + (weight_imag * source_imag - weight_real * source_real)
            part_ref[0, row] = real
            part_ref[1, row] = imag
            return carry

        lax.fori_loop(0, sites, near, 0)

        wait_all(turn)
        found = recv_ref[turn].T
        row_real, row_imag = found[:sites], found[sites : 2 * sites]
        col_real, col_imag = found[2 * sites : 3 * sites], found[3 * sites : 4 * sites]
        tl = (
            left_real * row_imag + left_imag * row_real,
            left_imag * row_imag - left_real * row_real,
        )
        tr_ref[0] = -(right_real * col_imag + right_imag * col_real)
        tr_ref[1] = right_real * col_real - right_imag * col_imag
        own_col = own_col_ref[...]
        blocks = [
            tl[part] * own_row_ref[row] + own_col * tr_ref[part, row : row + 1, :]
            for part in range(2)
            for row in range(sites)
        ]
        high, low = split(jnp.concatenate(blocks, axis=0))
        far = dot(jnp.concatenate([high, low], axis=1), place_ref[...])
        power_ref[turn] = part_ref[...] + far.reshape(2, sites, sites, owned)
        return carry

    turns = len(ERRORS)
    lax.fori_loop(1, turns + 1, advance, 0)

    def combine(poly):
        terms = [
            power_ref[k] if c == 1.0 else power_ref[k] * c for k, c in enumerate(poly) if c != 0.0
        ]
        return functools.reduce(jnp.add, terms)

    out_ref[...] = combine(NEW_POLY)
    scale = ABS_TOL + REL_TOL * jnp.maximum(jnp.abs(power_ref[0]), jnp.abs(out_ref[...]))
    ratio = combine(ERR_POLY) / scale
    tile = jnp.sum((ratio * ratio).reshape(2 * pairs // 8, 8, owned), axis=0)
    tile = jnp.sum(tile, axis=0, keepdims=True)
    tile = jnp.sum(tile, axis=1, keepdims=True)
    send_ref[...] = jnp.broadcast_to(tile, (asks, width))
    last = turns + 1
    send_all(last)
    wait_all(last)
    total = jnp.sum(recv_ref[last], axis=0, keepdims=True) * (1.0 / rows)
    entries = 2 * pairs * owned * peers
    norm_ref[...] = jnp.sqrt(total[:, :1] / entries)


def shards(
    state, hamiltonian, mode_rates, ado_modes, link_src, link_site, link_coef, send_ids, step_units
):
    groups = lax.axis_size("grp")
    members = lax.axis_size("dev")
    sites, owned = state.shape[1], state.shape[3]
    links = link_src.shape[0]
    received = send_ids.shape[1]
    asks = received * USES
    wide = links * owned
    pairs = sites * sites
    width = -(-4 * sites // 128) * 128
    turns = len(ERRORS) + 2
    vmem = pl.BlockSpec(memory_space=pltpu.VMEM)
    hbm = pl.BlockSpec(memory_space=pltpu.HBM)
    new_state, norm = pl.pallas_call(
        functools.partial(kernel, groups, members),
        out_shape=(
            jax.ShapeDtypeStruct(state.shape, F32),
            jax.ShapeDtypeStruct((1, 1), F32),
        ),
        in_specs=[hbm] * 9,
        out_specs=(vmem, vmem),
        scratch_shapes=[
            pltpu.VMEM(hamiltonian.shape, F32),
            pltpu.VMEM((1, mode_rates.shape[0]), F32),
            pltpu.VMEM(ado_modes.shape, jnp.int32),
            pltpu.VMEM(link_src.shape, jnp.int32),
            pltpu.VMEM(link_site.shape, jnp.int32),
            pltpu.VMEM(link_coef.shape, F32),
            pltpu.VMEM(send_ids.shape, jnp.int32),
            pltpu.SMEM((1, 1), jnp.int32),
            pltpu.VMEM((len(ERRORS) + 1,) + state.shape, F32),
            pltpu.VMEM(state.shape, F32),
            pltpu.VMEM((2 * pairs, pairs), BF16),
            pltpu.VMEM((2 * owned, asks), BF16),
            pltpu.VMEM((2 * owned, wide), BF16),
            pltpu.VMEM((asks, wide), F32),
            pltpu.VMEM((2 * asks, owned), BF16),
            pltpu.VMEM((2, sites, sites, wide), F32),
            pltpu.VMEM((sites, 1, asks), F32),
            pltpu.VMEM((sites, asks), F32),
            pltpu.VMEM((sites, 1, asks), F32),
            pltpu.VMEM((sites, asks), F32),
            pltpu.VMEM((2, sites, sites, asks), F32),
            pltpu.VMEM((2, sites, asks), F32),
            pltpu.VMEM((2 * pairs, 2 * owned), BF16),
            pltpu.VMEM((2, sites, sites, wide), F32),
            pltpu.VMEM((2, sites, asks), F32),
            pltpu.VMEM((asks, width), F32),
            pltpu.VMEM((turns, asks, width), F32),
            pltpu.SemaphoreType.DMA((9,)),
            pltpu.SemaphoreType.DMA((turns,)),
            pltpu.SemaphoreType.DMA((turns,)),
        ],
        compiler_params=pltpu.CompilerParams(
            collective_id=0, has_side_effects=True, vmem_limit_bytes=64 * 1024 * 1024
        ),
    )(
        state,
        hamiltonian,
        mode_rates.reshape(1, -1),
        ado_modes,
        link_src,
        link_site,
        link_coef,
        send_ids,
        step_units.reshape(1, 1),
    )
    return new_state, norm.reshape(())


def solution(mesh):
    return jax.shard_map(
        shards,
        mesh=mesh,
        in_specs=(
            P(None, None, None, ("grp", "dev")),
            P(),
            P(),
            P(None, ("grp", "dev")),
            P(None, ("grp", "dev")),
            P(None, ("grp", "dev")),
            P(None, None, ("grp", "dev")),
            P(("grp", "dev"), None),
            P(),
        ),
        out_specs=(P(None, None, None, ("grp", "dev")), P()),
        check_vma=False,
    )
```

time: 81.9 us -> 73 us (0.89)
  Pallas kernels: 74.3 us -> 67.8 us
  local copies, waits for them, and re-layouts: 5.83 us -> 1.92 us
  between operations: 1.34 us -> 3.09 us
    pallas_call x1, Pallas kernels: 74.3 us -> 67.8 us  [shards(): pl.pallas_call(functools.partial(kernel, groups, members), out_shape=(jax...]
    unnamed x17 -> x1, local copies, waits for them, and re-layouts: 5.32 us -> 1.92 us
where the time goes in v2:
time: 73 us; the launch traced here: 72.8 us
  Pallas kernels  67.8 us (93%)
  between operations  3.09 us (4%)
  local copies, waits for them, and re-layouts  1.92 us (3%)
    pallas_call x1, Pallas kernels, shards(): pl.pallas_call(functools.partial(kernel, groups, members), out_shape=(jax...  67.8 us
    unnamed x1, local copies, waits for them, and re-layouts  1.92 us

profile of v2, /device:TPU:0, one launch (start us, length us, event | category | flops | bytes accessed | tf_op | source)
XLA Modules:
  0.0 72.8 jit_solution(3688045265101822062)
XLA Ops:
  1.3 67.8 %shard_map.104 = (f32[2,24,24,128]{3,2,1,0:T(8,128)}, f32[1,1]{1,0:T(1,128)}) custom-call(f32[2,24,24,128]{3,2,1,0:T(8,128)} %state_hbm.1, f32[24,24]{1,0:T(8,128)} %ham_hbm.1, f32[1,96]{1,0:T(1,128)} %bitcast.4, s32[3,128]{1,0:T(4,128)} %modes_hbm.1, s32[8,128]{1,0:T(8,128)} %src_hbm.1, s32[8,128]{1,0:T(8,128)} %site_hbm.1, f32[4,8,128]{2,1,0:T(8,128)} %coef_hbm.1, ...), custom_call_target="tpu_custom_call" | custom-call | tf_op jit(solution)/shard_map/pallas_call | solution.py:398
  69.1 1.9 %copy.14 = f32[2,24,24,128]{3,2,1,0:T(8,128)} copy(f32[2,24,24,128]{3,2,1,0:T(8,128)} %get-tuple-element.8) | data formatting | bytes 1179648

commit v3 on v2

--- a/solution.py
+++ b/solution.py
@@ -115,9 +115,13 @@
     tr_ref,
     send_ref,
     recv_ref,
+    note_ref,
+    noted_ref,
     load_sem,
     send_sem,
     recv_sem,
+    note_send_sem,
+    note_recv_sem,
 ):
     peers = groups * members
     sites = state_hbm.shape[1]
@@ -135,7 +139,7 @@
     def wrap(value, size):
         return jnp.where(value >= size, value - size, value)
 
-    def each_peer(visit):
+    def each_peer(visit, unroll=False):
         for jump in range(1, groups):
             visit(wrap(my_grp + jump, groups), my_dev)
 
@@ -145,7 +149,11 @@
                 visit(wrap(my_grp + jump, groups), dev)
             return carry
 
-        lax.fori_loop(1, members, ring, 0)
+        if unroll:
+            for step in range(1, members):
+                ring(step, 0)
+        else:
+            lax.fori_loop(1, members, ring, 0)
 
     barrier = pltpu.get_barrier_semaphore()
 
@@ -179,23 +187,44 @@
             peer = grp * members + dev
             pltpu.make_async_remote_copy(
                 src_ref=send_ref.at[pl.ds(pl.multiple_of(peer * rows, rows), rows)],
-                dst_ref=recv_ref.at[turn, mine],
-                send_sem=send_sem.at[turn],
-                recv_sem=recv_sem.at[turn],
+                dst_ref=recv_ref.at[turn - 1, mine],
+                send_sem=send_sem.at[turn - 1],
+                recv_sem=recv_sem.at[turn - 1],
                 device_id=(grp, dev),
                 device_id_type=MESH,
             ).start()
 
-        each_peer(send)
-        recv_ref[turn, mine] = send_ref[mine]
+        each_peer(send, unroll=True)
+        recv_ref[turn - 1, mine] = send_ref[mine]
 
     def bulk(turn, sem):
         every = pl.ds(0, (peers - 1) * rows)
         return pltpu.make_async_copy(send_ref.at[every], recv_ref.at[turn, every], sem.at[turn])
 
     def wait_all(turn):
-        bulk(turn, recv_sem).wait()
-        bulk(turn, send_sem).wait()
+        bulk(turn - 1, recv_sem).wait()
+        bulk(turn - 1, send_sem).wait()
+
+    def send_note(note):
+        def send(grp, dev):
+            pltpu.make_async_remote_copy(
+                src_ref=note_ref.at[note, grp * members + dev],
+                dst_ref=noted_ref.at[note, me],
+                send_sem=note_send_sem.at[note],
+                recv_sem=note_recv_sem.at[note],
+                device_id=(grp, dev),
+                device_id_type=MESH,
+            ).start()
+
+        each_peer(send)
+        noted_ref[note, me] = note_ref[note, me]
+
+    def wait_note(note):
+        every = pl.ds(0, peers - 1)
+        for sem in (note_recv_sem, note_send_sem):
+            pltpu.make_async_copy(
+                note_ref.at[note, every], noted_ref.at[note, every], sem.at[note]
+            ).wait()
 
     earlier = one_hot(iota((owned, owned), 0) < iota((owned, owned), 1), BF16)
     base = jnp.zeros((received, 1), F32)
@@ -221,9 +250,15 @@
         local = one_hot(iota((owned, owned), 0) == source, BF16)
         select_ref[:owned, lanes] = local
         select_ref[owned:, lanes] = local
-    send_ref[...] = jnp.broadcast_to(jnp.sum(wanted, axis=1, keepdims=True), (asks, width))
+    lane_of = iota((peers, rows, 128), 1) == iota((peers, rows, 128), 2)
+    lane_of = one_hot(lane_of, F32).reshape(asks, 128)
+    peer_of = iota((peers, rows, peers), 0) == iota((peers, rows, peers), 2)
+    peer_of = one_hot(peer_of, F32).reshape(asks, peers)
+    wanted = jnp.sum(wanted, axis=1, keepdims=True) * lane_of
+    wanted = wanted.reshape(peers, rows, 128).sum(axis=1, keepdims=True)
+    note_ref[0] = wanted
     pl.semaphore_wait(barrier, peers - 1)
-    send_all(0)
+    send_note(0)
 
     place_ref[:asks] = place.astype(BF16)
     place_ref[asks:] = place.astype(BF16)
@@ -282,8 +317,10 @@
     pick_ref[:owned] = picks
     pick_ref[owned:] = picks
 
-    wait_all(0)
-    asked = recv_ref[0].T[0:1].astype(jnp.int32)
+    wait_note(0)
+    asked = dot(peer_of.astype(BF16), noted_ref[0].reshape(peers, 128).astype(BF16))
+    asked = jnp.broadcast_to(jnp.sum(asked * lane_of, axis=1, keepdims=True), (asks, 128))
+    asked = asked.T[0:1].astype(jnp.int32)
     asked_col_ref[...] = one_hot(iota((sites, asks), 0) == asked, F32)
     asked_row_ref[...] = one_hot(iota((sites, 1, asks), 0) == asked[None], F32)
 
@@ -336,7 +373,7 @@
         lax.fori_loop(0, sites, near, 0)
 
         wait_all(turn)
-        found = recv_ref[turn].T
+        found = recv_ref[turn - 1].T
         row_real, row_imag = found[:sites], found[sites : 2 * sites]
         col_real, col_imag = found[2 * sites : 3 * sites], found[3 * sites : 4 * sites]
         tl = (
@@ -365,17 +402,18 @@
         ]
         return functools.reduce(jnp.add, terms)
 
-    out_ref[...] = combine(NEW_POLY)
-    scale = ABS_TOL + REL_TOL * jnp.maximum(jnp.abs(power_ref[0]), jnp.abs(out_ref[...]))
+    increment = combine([0.0] + NEW_POLY[1:])
+    out_ref[...] = increment
+    new_state = power_ref[0] + increment
+    scale = ABS_TOL + REL_TOL * jnp.maximum(jnp.abs(power_ref[0]), jnp.abs(new_state))
     ratio = combine(ERR_POLY) / scale
     tile = jnp.sum((ratio * ratio).reshape(2 * pairs // 8, 8, owned), axis=0)
     tile = jnp.sum(tile, axis=0, keepdims=True)
     tile = jnp.sum(tile, axis=1, keepdims=True)
-    send_ref[...] = jnp.broadcast_to(tile, (asks, width))
-    last = turns + 1
-    send_all(last)
-    wait_all(last)
-    total = jnp.sum(recv_ref[last], axis=0, keepdims=True) * (1.0 / rows)
+    note_ref[1] = jnp.broadcast_to(tile[None], (peers, 1, 128))
+    send_note(1)
+    wait_note(1)
+    total = jnp.sum(noted_ref[1], axis=0)
     entries = 2 * pairs * owned * peers
     norm_ref[...] = jnp.sqrt(total[:, :1] / entries)
 
@@ -392,10 +430,10 @@
     wide = links * owned
     pairs = sites * sites
     width = -(-4 * sites // 128) * 128
-    turns = len(ERRORS) + 2
+    turns = len(ERRORS)
     vmem = pl.BlockSpec(memory_space=pltpu.VMEM)
     hbm = pl.BlockSpec(memory_space=pltpu.HBM)
-    new_state, norm = pl.pallas_call(
+    increment, norm = pl.pallas_call(
         functools.partial(kernel, groups, members),
         out_shape=(
             jax.ShapeDtypeStruct(state.shape, F32),
@@ -431,9 +469,13 @@
             pltpu.VMEM((2, sites, asks), F32),
             pltpu.VMEM((asks, width), F32),
             pltpu.VMEM((turns, asks, width), F32),
+            pltpu.VMEM((2, groups * members, 1, 128), F32),
+            pltpu.VMEM((2, groups * members, 1, 128), F32),
             pltpu.SemaphoreType.DMA((9,)),
             pltpu.SemaphoreType.DMA((turns,)),
             pltpu.SemaphoreType.DMA((turns,)),
+            pltpu.SemaphoreType.DMA((2,)),
+            pltpu.SemaphoreType.DMA((2,)),
         ],
         compiler_params=pltpu.CompilerParams(
             collective_id=0, has_side_effects=True, vmem_limit_bytes=64 * 1024 * 1024
@@ -449,7 +491,7 @@
         send_ids,
         step_units.reshape(1, 1),
     )
-    return new_state, norm.reshape(())
+    return state + increment, norm.reshape(())
 
 
 def solution(mesh):

time: 73 us -> 73.2 us (level)
  other arithmetic: 0 us -> 2.12 us
  local copies, waits for them, and re-layouts: 1.92 us -> 0 us
    add x0 -> x1, other arithmetic: none -> 2.12 us  [shards(): return (state + increment, norm.reshape(()))]
    unnamed x1 -> x0, local copies, waits for them, and re-layouts: 1.92 us -> none
where the time goes in v3:
time: 73.2 us; the launch traced here: 72.9 us
  Pallas kernels  67.7 us (92%)
  between operations  3.09 us (4%)
  other arithmetic  2.12 us (3%)
    pallas_call x1, Pallas kernels, shards(): pl.pallas_call(functools.partial(kernel, groups, members), out_shape=(jax...  67.7 us
    add x1, other arithmetic, shards(): return (state + increment, norm.reshape(()))  2.12 us

profile of v3, /device:TPU:0, one launch (start us, length us, event | category | flops | bytes accessed | tf_op | source)
XLA Modules:
  0.0 72.9 jit_solution(14471521161419403338)
XLA Ops:
  1.3 67.7 %shard_map.104 = (f32[2,24,24,128]{3,2,1,0:T(8,128)}, f32[1,1]{1,0:T(1,128)}) custom-call(f32[2,24,24,128]{3,2,1,0:T(8,128)} %state_hbm.1, f32[24,24]{1,0:T(8,128)} %ham_hbm.1, f32[1,96]{1,0:T(1,128)} %bitcast.4, s32[3,128]{1,0:T(4,128)} %modes_hbm.1, s32[8,128]{1,0:T(8,128)} %src_hbm.1, s32[8,128]{1,0:T(8,128)} %site_hbm.1, f32[4,8,128]{2,1,0:T(8,128)} %coef_hbm.1, ...), custom_call_target="tpu_custom_call" | custom-call | tf_op jit(solution)/shard_map/pallas_call | solution.py:436
  69.0 2.1 %add.3 = f32[2,24,24,128]{3,2,1,0:T(8,128)} add(f32[2,24,24,128]{3,2,1,0:T(8,128)} %state_hbm.1, f32[2,24,24,128]{3,2,1,0:T(8,128)} %get-tuple-element.4) | non-fusion elementwise | flops 147456 | bytes 1769472 | tf_op jit(solution)/shard_map/add | solution.py:494

commit v4 on v3

--- a/solution.py
+++ b/solution.py
@@ -102,7 +102,7 @@
     pick_ref,
     select_ref,
     request_ref,
-    place_ref,
+    spread_ref,
     weight_ref,
     own_row_ref,
     own_col_ref,
@@ -111,6 +111,7 @@
     chosen_ref,
     cols_ref,
     halves_ref,
+    arrived_ref,
     fetched_ref,
     tr_ref,
     send_ref,
@@ -172,7 +173,7 @@
                 (rates_hbm, rates_ref),
                 (modes_hbm, modes_ref),
                 (ids_hbm, ids_ref),
-                (state_hbm, power_ref.at[0]),
+                (state_hbm, part_ref),
             )
         )
     ]
@@ -260,8 +261,9 @@
     pl.semaphore_wait(barrier, peers - 1)
     send_note(0)
 
-    place_ref[:asks] = place.astype(BF16)
-    place_ref[asks:] = place.astype(BF16)
+    place = place.astype(BF16)
+    for start in (0, asks):
+        spread_ref[start : start + asks, asks:] = place
     for load in loads[2:]:
         load.wait()
     step_size = units_ref[0, 0].astype(F32) * UNIT_STEP
@@ -288,16 +290,21 @@
                 weight_ref[part, row, :, lanes] = jnp.where(site == row, left, 0.0) - right
     first = one_hot(iota((sites, sites, sites), 0) == iota((sites, sites, sites), 2), F32)
     second = one_hot(iota((sites, sites, sites), 1) == iota((sites, sites, sites), 2), F32)
-    first, second = first.reshape(pairs, sites), second.reshape(pairs, sites)
+    first, second = (hot.reshape(pairs, sites).astype(BF16) for hot in (first, second))
     ham = ham_ref[...] * (0.5 * step_size)
 
+    def pieces(values):
+        high, low = split(values)
+        middle = high.astype(F32) + low.astype(F32)
+        return high, low, (values - middle).astype(BF16)
+
     def lifted(hot):
-        half = jnp.dot(hot, ham, precision=HIGHEST, preferred_element_type=F32)
-        half = half + dot_nt(hot, ham, HIGHEST)
-        return dot_nt(half, hot, HIGHEST)
-
-    same_first = dot_nt(first.astype(BF16), first.astype(BF16))
-    same_second = dot_nt(second.astype(BF16), second.astype(BF16))
+        half = functools.reduce(
+            jnp.add, [dot(hot, piece) + dot_nt(hot, piece) for piece in pieces(ham)]
+        )
+        return functools.reduce(jnp.add, [dot_nt(piece, hot) for piece in pieces(half)])
+
+    same_first, same_second = dot_nt(first, first), dot_nt(second, second)
     operator = lifted(first) * same_second - lifted(second) * same_first
     high, low = split(operator)
     super_ref[:pairs] = high
@@ -316,6 +323,18 @@
     picks = one_hot(iota((owned, asks), 0) == ids, BF16)
     pick_ref[:owned] = picks
     pick_ref[owned:] = picks
+    relay = dot(place, picks).astype(BF16)
+    for start in (0, asks):
+        spread_ref[start : start + asks, :asks] = relay
+
+    def prepare():
+        high, low = split(part_ref[...].reshape(2 * pairs, owned))
+        chosen_ref[...] = dot(jnp.concatenate([high, low], axis=1), pick_ref[...]).reshape(
+            2, sites, sites, asks
+        )
+
+    prepare()
+    arrived_ref[...] = jnp.zeros(arrived_ref.shape, BF16)
 
     wait_note(0)
     asked = dot(peer_of.astype(BF16), noted_ref[0].reshape(peers, 128).astype(BF16))
@@ -326,15 +345,13 @@
 
     def advance(turn, carry):
         before = turn - 1
-        high, low = split(power_ref[before].reshape(2 * pairs, owned))
-        halves_ref[...] = jnp.concatenate([high, low], axis=1)
-        chosen_ref[...] = dot(halves_ref[...], pick_ref[...]).reshape(2, sites, sites, asks)
+        relayed = dot(arrived_ref[...], spread_ref[:, :asks]).reshape(2, sites, sites, asks)
         col_mask = asked_col_ref[...]
         picked = []
         for part in range(2):
             total = jnp.zeros((sites, asks), F32)
             for row in range(sites):
-                block = chosen_ref[part, row]
+                block = chosen_ref[part, row] + relayed[part, row]
                 total = total + block * asked_row_ref[row]
                 cols_ref[part, row : row + 1, :] = jnp.sum(block * col_mask, axis=0, keepdims=True)
             picked.append(total)
@@ -346,6 +363,11 @@
         send_ref[...] = outgoing.T
         send_all(turn)
 
+        far = dot(arrived_ref[...], spread_ref[:, asks:]).reshape(2, sites, sites, owned)
+        current = part_ref[...] + far
+        power_ref[before] = current
+        high, low = split(current.reshape(2 * pairs, owned))
+        halves_ref[...] = jnp.concatenate([high, low], axis=1)
         fetched_ref[...] = dot(halves_ref[...], select_ref[...]).reshape(2, sites, sites, wide)
         high = jnp.concatenate([halves_ref[:pairs, :owned], halves_ref[pairs:, :owned]], axis=1)
         low = jnp.concatenate([halves_ref[:pairs, owned:], halves_ref[pairs:, owned:]], axis=1)
@@ -371,6 +393,7 @@
             return carry
 
         lax.fori_loop(0, sites, near, 0)
+        prepare()
 
         wait_all(turn)
         found = recv_ref[turn - 1].T
@@ -389,12 +412,13 @@
             for row in range(sites)
         ]
         high, low = split(jnp.concatenate(blocks, axis=0))
-        far = dot(jnp.concatenate([high, low], axis=1), place_ref[...])
-        power_ref[turn] = part_ref[...] + far.reshape(2, sites, sites, owned)
+        arrived_ref[...] = jnp.concatenate([high, low], axis=1)
         return carry
 
     turns = len(ERRORS)
     lax.fori_loop(1, turns + 1, advance, 0)
+    far = dot(arrived_ref[...], spread_ref[:, asks:]).reshape(2, sites, sites, owned)
+    power_ref[turns] = part_ref[...] + far
 
     def combine(poly):
         terms = [
@@ -456,7 +480,7 @@
             pltpu.VMEM((2 * owned, asks), BF16),
             pltpu.VMEM((2 * owned, wide), BF16),
             pltpu.VMEM((asks, wide), F32),
-            pltpu.VMEM((2 * asks, owned), BF16),
+            pltpu.VMEM((2 * asks, asks + owned), BF16),
             pltpu.VMEM((2, sites, sites, wide), F32),
             pltpu.VMEM((sites, 1, asks), F32),
             pltpu.VMEM((sites, asks), F32),
@@ -465,6 +489,7 @@
             pltpu.VMEM((2, sites, sites, asks), F32),
             pltpu.VMEM((2, sites, asks), F32),
             pltpu.VMEM((2 * pairs, 2 * owned), BF16),
+            pltpu.VMEM((2 * pairs, 2 * asks), BF16),
             pltpu.VMEM((2, sites, sites, wide), F32),
             pltpu.VMEM((2, sites, asks), F32),
             pltpu.VMEM((asks, width), F32),

time: 73.2 us -> 70.4 us (0.962)
  Pallas kernels: 67.7 us -> 65 us
    pallas_call x1, Pallas kernels: 67.7 us -> 65 us  [shards(): pl.pallas_call(functools.partial(kernel, groups, members), out_shape=(jax...]
where the time goes in v4:
time: 70.4 us; the launch traced here: 70.2 us
  Pallas kernels  65 us (92%)
  between operations  3.09 us (4%)
  other arithmetic  2.12 us (3%)
    pallas_call x1, Pallas kernels, shards(): pl.pallas_call(functools.partial(kernel, groups, members), out_shape=(jax...  65 us
    add x1, other arithmetic, shards(): return (state + increment, norm.reshape(()))  2.12 us

profile of v4, /device:TPU:0, one launch (start us, length us, event | category | flops | bytes accessed | tf_op | source)
XLA Modules:
  0.0 70.2 jit_solution(11468547728626069623)
XLA Ops:
  1.3 65.0 %shard_map.104 = (f32[2,24,24,128]{3,2,1,0:T(8,128)}, f32[1,1]{1,0:T(1,128)}) custom-call(f32[2,24,24,128]{3,2,1,0:T(8,128)} %state_hbm.1, f32[24,24]{1,0:T(8,128)} %ham_hbm.1, f32[1,96]{1,0:T(1,128)} %bitcast.4, s32[3,128]{1,0:T(4,128)} %modes_hbm.1, s32[8,128]{1,0:T(8,128)} %src_hbm.1, s32[8,128]{1,0:T(8,128)} %site_hbm.1, f32[4,8,128]{2,1,0:T(8,128)} %coef_hbm.1, ...), custom_call_target="tpu_custom_call" | custom-call | tf_op jit(solution)/shard_map/pallas_call | solution.py:460
  66.3 2.1 %add.3 = f32[2,24,24,128]{3,2,1,0:T(8,128)} add(f32[2,24,24,128]{3,2,1,0:T(8,128)} %state_hbm.1, f32[2,24,24,128]{3,2,1,0:T(8,128)} %get-tuple-element.4) | non-fusion elementwise | flops 147456 | bytes 1769472 | tf_op jit(solution)/shard_map/add | solution.py:519

commit v5 on v4

--- a/solution.py
+++ b/solution.py
@@ -25,6 +25,16 @@
 MESH = pl.DeviceIdType.MESH
 F32 = jnp.float32
 BF16 = jnp.bfloat16
+
+
+def folding(rows, values, width):
+    spare = width - values
+    pieces = values // spare if spare else 0
+    if not pieces or values % spare:
+        return rows, 0, ()
+    dropped = rows // (pieces + 1)
+    kept = rows - dropped
+    return kept, spare, [(k, kept + k // pieces, k % pieces) for k in range(dropped * pieces)]
 
 
 def step_polynomials():
@@ -115,6 +125,7 @@
     fetched_ref,
     tr_ref,
     send_ref,
+    full_ref,
     recv_ref,
     note_ref,
     noted_ref,
@@ -133,7 +144,9 @@
     asks = received * USES
     rows = asks // peers
     pairs = sites * sites
-    width = send_ref.shape[1]
+    width = send_ref.shape[2]
+    kept, spare, moves = folding(rows, 4 * sites, width)
+    turn_of_lane = lax.rem(iota((max(spare, 1), asks), 1), rows)
     my_grp, my_dev = lax.axis_index("grp"), lax.axis_index("dev")
     me = my_grp * members + my_dev
 
@@ -182,13 +195,10 @@
     each_peer(greet)
 
     def send_all(turn):
-        mine = pl.ds(pl.multiple_of(me * rows, rows), rows)
-
         def send(grp, dev):
-            peer = grp * members + dev
             pltpu.make_async_remote_copy(
-                src_ref=send_ref.at[pl.ds(pl.multiple_of(peer * rows, rows), rows)],
-                dst_ref=recv_ref.at[turn - 1, mine],
+                src_ref=send_ref.at[grp * members + dev],
+                dst_ref=recv_ref.at[turn - 1, me],
                 send_sem=send_sem.at[turn - 1],
                 recv_sem=recv_sem.at[turn - 1],
                 device_id=(grp, dev),
@@ -196,10 +206,10 @@
             ).start()
 
         each_peer(send, unroll=True)
-        recv_ref[turn - 1, mine] = send_ref[mine]
+        recv_ref[turn - 1, me] = send_ref[me]
 
     def bulk(turn, sem):
-        every = pl.ds(0, (peers - 1) * rows)
+        every = pl.ds(0, peers - 1)
         return pltpu.make_async_copy(send_ref.at[every], recv_ref.at[turn, every], sem.at[turn])
 
     def wait_all(turn):
@@ -335,6 +345,7 @@
 
     prepare()
     arrived_ref[...] = jnp.zeros(arrived_ref.shape, BF16)
+    full_ref[...] = jnp.zeros(full_ref.shape, F32)
 
     wait_note(0)
     asked = dot(peer_of.astype(BF16), noted_ref[0].reshape(peers, 128).astype(BF16))
@@ -355,12 +366,15 @@
                 total = total + block * asked_row_ref[row]
                 cols_ref[part, row : row + 1, :] = jnp.sum(block * col_mask, axis=0, keepdims=True)
             picked.append(total)
-        outgoing = jnp.concatenate(
-            picked
-            + [cols_ref[...].reshape(2 * sites, asks), jnp.zeros((width - 4 * sites, asks), F32)],
-            axis=0,
-        )
-        send_ref[...] = outgoing.T
+        outgoing = jnp.concatenate(picked + [cols_ref[...].reshape(2 * sites, asks)], axis=0)
+        if spare:
+            extra = jnp.zeros((spare, asks), F32)
+            for keep, drop, piece in moves:
+                moved = outgoing[piece * spare : (piece + 1) * spare]
+                moved = pltpu.roll(moved, asks - (drop - keep), 1)
+                extra = jnp.where(turn_of_lane == keep, moved, extra)
+            outgoing = jnp.concatenate([outgoing, extra], axis=0)
+        send_ref[...] = outgoing.T.reshape(peers, rows, width)[:, :kept]
         send_all(turn)
 
         far = dot(arrived_ref[...], spread_ref[:, asks:]).reshape(2, sites, sites, owned)
@@ -396,7 +410,15 @@
         prepare()
 
         wait_all(turn)
-        found = recv_ref[turn - 1].T
+        full_ref[:, :kept] = recv_ref[turn - 1]
+        found = full_ref[...].reshape(asks, width).T
+        if spare:
+            extra = found[4 * sites :]
+            parts = [found[k : k + spare] for k in range(0, 4 * sites, spare)]
+            for keep, drop, piece in moves:
+                moved = pltpu.roll(extra, drop - keep, 1)
+                parts[piece] = jnp.where(turn_of_lane == drop, moved, parts[piece])
+            found = jnp.concatenate(parts, axis=0)
         row_real, row_imag = found[:sites], found[sites : 2 * sites]
         col_real, col_imag = found[2 * sites : 3 * sites], found[3 * sites : 4 * sites]
         tl = (
@@ -454,6 +476,9 @@
     wide = links * owned
     pairs = sites * sites
     width = -(-4 * sites // 128) * 128
+    peers = groups * members
+    rows = asks // peers
+    kept, _, _ = folding(rows, 4 * sites, width)
     turns = len(ERRORS)
     vmem = pl.BlockSpec(memory_space=pltpu.VMEM)
     hbm = pl.BlockSpec(memory_space=pltpu.HBM)
@@ -492,10 +517,11 @@
             pltpu.VMEM((2 * pairs, 2 * asks), BF16),
             pltpu.VMEM((2, sites, sites, wide), F32),
             pltpu.VMEM((2, sites, asks), F32),
-            pltpu.VMEM((asks, width), F32),
-            pltpu.VMEM((turns, asks, width), F32),
-            pltpu.VMEM((2, groups * members, 1, 128), F32),
-            pltpu.VMEM((2, groups * members, 1, 128), F32),
+            pltpu.VMEM((peers, kept, width), F32),
+            pltpu.VMEM((peers, rows, width), F32),
+            pltpu.VMEM((turns, peers, kept, width), F32),
+            pltpu.VMEM((2, peers, 1, 128), F32),
+            pltpu.VMEM((2, peers, 1, 128), F32),
             pltpu.SemaphoreType.DMA((9,)),
             pltpu.SemaphoreType.DMA((turns,)),
             pltpu.SemaphoreType.DMA((turns,)),

time: 70.4 us -> 68.6 us (0.974)
  Pallas kernels: 65 us -> 63.2 us
    pallas_call x1, Pallas kernels: 65 us -> 63.2 us  [shards(): pl.pallas_call(functools.partial(kernel, groups, members), out_shape=(jax...]
where the time goes in v5:
time: 68.6 us; the launch traced here: 68.4 us
  Pallas kernels  63.2 us (92%)
  between operations  3.09 us (5%)
  other arithmetic  2.12 us (3%)
    pallas_call x1, Pallas kernels, shards(): pl.pallas_call(functools.partial(kernel, groups, members), out_shape=(jax...  63.2 us
    add x1, other arithmetic, shards(): return (state + increment, norm.reshape(()))  2.12 us

profile of v5, /device:TPU:0, one launch (start us, length us, event | category | flops | bytes accessed | tf_op | source)
XLA Modules:
  0.0 68.4 jit_solution(8569562058559618899)
XLA Ops:
  1.3 63.2 %shard_map.104 = (f32[2,24,24,128]{3,2,1,0:T(8,128)}, f32[1,1]{1,0:T(1,128)}) custom-call(f32[2,24,24,128]{3,2,1,0:T(8,128)} %state_hbm.1, f32[24,24]{1,0:T(8,128)} %ham_hbm.1, f32[1,96]{1,0:T(1,128)} %bitcast.4, s32[3,128]{1,0:T(4,128)} %modes_hbm.1, s32[8,128]{1,0:T(8,128)} %src_hbm.1, s32[8,128]{1,0:T(8,128)} %site_hbm.1, f32[4,8,128]{2,1,0:T(8,128)} %coef_hbm.1, ...), custom_call_target="tpu_custom_call" | custom-call | tf_op jit(solution)/shard_map/pallas_call | solution.py:485
  64.4 2.1 %add.3 = f32[2,24,24,128]{3,2,1,0:T(8,128)} add(f32[2,24,24,128]{3,2,1,0:T(8,128)} %state_hbm.1, f32[2,24,24,128]{3,2,1,0:T(8,128)} %get-tuple-element.4) | non-fusion elementwise | flops 147456 | bytes 1769472 | tf_op jit(solution)/shard_map/add | solution.py:545
